TPU v7x, 32 devices: a whole 2x2x4 slice. The times are simulated.
32 devices in a mesh: patch: 8 (over y, x, core), mlp: 4 (over z).
Axes of the slice: x: 2, y: 2, z: 4, core: 2. Of those that a mesh axis runs over, the one named last changes fastest.
Arguments:
- latent: bfloat16 [2048, 2432], P('patch', 'mlp'), may hold values from -24 to 24
- split_list: int32 [8, 4], P('patch'), may hold values from 0 to 256, as said below
- modulation: float32 [1, 6, 2432], replicated, may hold values from -3 to 3
- w_qkv: bfloat16 [2432, 3, 1536], P(None, None, 'mlp'), may hold values from -0.125 to 0.125
- w_out: bfloat16 [1536, 2432], P('mlp'), may hold values from -0.15625 to 0.15625
- w_up: bfloat16 [2432, 5120], P(None, 'mlp'), may hold values from -0.125 to 0.125
- w_down: bfloat16 [5120, 2432], P('mlp'), may hold values from -0.078125 to 0.078125
- qk_gains: float32 [3, 64], replicated, may hold values from 1.6 to 2.4
- text_kv: bfloat16 [2, 1, 154, 1536], P(None, None, None, 'mlp'), may hold values from -6 to 6
- timestep: int32 [1], replicated, may hold values from 0 to 27
- step_sizes: float32 [28], replicated, may hold values from -0.6 to -0.1
Outputs:
- latent_next: bfloat16 [2048, 2432], P('patch', 'mlp')
Inputs may be any that keep to these rules, and one draw needn't show every extreme that they name: `split_list`: row d holds device d's tile pieces (item, count, item, count); over all devices the counts of every item add up to 1024. A device's two counts add up to at most 256, to exactly 256 on some device and to 0 on another. The devices holding an item's tokens form a run of consecutive indices of patch, taken cyclically. Both pieces may name the same item; they are then two parts of it.
All inputs are finite; a program needn't handle non-finite values.
Results may differ from a plain program's by a relative error of at most 0.0049.
Values may be sent and summed in bfloat16 or wider, within the bound.
A program may use at most 128 MiB of HBM per device.

v0:
```python
import jax
import jax.numpy as jnp
from jax import lax
from jax.sharding import PartitionSpec as P

HEAD = 64
norm_eps = 1e-06
block_rows = 512


def layer_norm(row_data):
    row_mean = jnp.mean(row_data, axis=-1, keepdims=True)
    centred = row_data - row_mean
    variance = jnp.mean(centred * centred, axis=-1, keepdims=True)
    return centred * lax.rsqrt(variance + norm_eps)


def head_norm(row_data, gain_row):
    shaped = row_data.reshape(row_data.shape[0], -1, HEAD)
    mean_square = jnp.mean(shaped * shaped, axis=-1, keepdims=True)
    return (shaped * lax.rsqrt(mean_square + norm_eps) * gain_row).reshape(row_data.shape)


def attend_dense(state_pair, queries, query_tags, key_rows, value_rows, key_tags):
    numerator, denominator = state_pair
    query_count = queries.shape[0]
    heads_here = queries.shape[1] // HEAD
    query_heads = queries.reshape(query_count, heads_here, HEAD)
    key_heads = key_rows.reshape(key_rows.shape[0], heads_here, HEAD)
    value_heads = value_rows.reshape(value_rows.shape[0], heads_here, HEAD)
    scores = jnp.einsum(
        "qhd,khd->qhk", query_heads, key_heads, preferred_element_type=jnp.float32
    ) * HEAD ** (-0.5)
    same_item = (query_tags[:, None] == key_tags[None, :])[:, None, :]
    weights = jnp.where(same_item, jnp.exp(scores), 0.0)
    denominator = denominator + jnp.sum(weights, axis=-1)
    numerator = numerator + jnp.einsum(
        "qhk,khd->qhd",
        weights.astype(jnp.bfloat16),
        value_heads,
        preferred_element_type=jnp.float32,
    )
    return (numerator, denominator)


def attend_block(state_pair, queries, query_tags, key_rows, value_rows, key_tags):
    touching = jnp.any(query_tags[:, None] == key_tags[None, :])

    def work(inner):
        return attend_dense(inner, queries, query_tags, key_rows, value_rows, key_tags)

    def skip(inner):
        return inner

    return lax.cond(touching, work, skip, state_pair)


def attend(state_pair, queries, query_tags, key_rows, value_rows, key_tags):
    key_count = key_rows.shape[0]
    if key_count > 2 * block_rows and key_count % block_rows == 0:

        def one_block(block_index, inner):
            offset = block_index * block_rows
            return attend_block(
                inner,
                queries,
                query_tags,
                lax.dynamic_slice_in_dim(key_rows, offset, block_rows, 0),
                lax.dynamic_slice_in_dim(value_rows, offset, block_rows, 0),
                lax.dynamic_slice_in_dim(key_tags, offset, block_rows, 0),
            )

        return lax.fori_loop(0, key_count // block_rows, one_block, state_pair)
    return attend_block(state_pair, queries, query_tags, key_rows, value_rows, key_tags)


def body(
    latent,
    split_list,
    modulation,
    w_qkv,
    w_out,
    w_up,
    w_down,
    qk_gains,
    text_kv,
    timestep,
    step_sizes,
):
    share_cols = latent.shape[1]
    row_data = lax.all_gather(latent, "mlp", axis=1, tiled=True)
    capacity = row_data.shape[0]
    item_total = modulation.shape[0]
    item_a = split_list[0, 0]
    count_a = split_list[0, 1]
    item_b = split_list[0, 2]
    count_b = split_list[0, 3]
    slot_ids = jnp.arange(capacity, dtype=jnp.int32)
    in_first = slot_ids < count_a
    slot_live = slot_ids < count_a + count_b
    slot_item = jnp.where(in_first, item_a, jnp.where(slot_live, item_b, -1))
    item_ids = jnp.arange(item_total, dtype=jnp.int32)
    one_hot = (slot_item[:, None] == item_ids[None, :]).astype(jnp.float32)
    slot_mods = jnp.dot(
        one_hot,
        modulation.reshape(item_total, -1),
        precision=lax.Precision.HIGHEST,
        preferred_element_type=jnp.float32,
    ).reshape(capacity, 6, -1)
    slot_step = jnp.dot(
        one_hot,
        jnp.take(step_sizes, timestep),
        precision=lax.Precision.HIGHEST,
        preferred_element_type=jnp.float32,
    )
    float_rows = row_data.astype(jnp.float32)
    normed_one = (layer_norm(float_rows) * (1.0 + slot_mods[:, 1]) + slot_mods[:, 0]).astype(
        jnp.bfloat16
    )
    projected = jnp.einsum("nd,dch->nch", normed_one, w_qkv, preferred_element_type=jnp.float32)
    queries = head_norm(projected[:, 0], qk_gains[0]).astype(jnp.bfloat16)
    key_rows = head_norm(projected[:, 1], qk_gains[1]).astype(jnp.bfloat16)
    value_rows = projected[:, 2].astype(jnp.bfloat16)
    head_cols = queries.shape[1]
    heads_here = head_cols // HEAD
    text_pair = jnp.take(text_kv, jnp.stack([item_a, item_b]), axis=1)
    text_keys = head_norm(
        text_pair[0].reshape(-1, head_cols).astype(jnp.float32), qk_gains[2]
    ).astype(jnp.bfloat16)
    text_values = text_pair[1].reshape(-1, head_cols)
    second_tag = jnp.where(item_b != item_a, item_b, -2)
    text_tags = jnp.repeat(jnp.stack([item_a, second_tag]), text_kv.shape[2]).astype(jnp.bfloat16)
    query_tags = slot_item.astype(jnp.bfloat16)
    key_tags = jnp.where(slot_live, slot_item, -3).astype(jnp.bfloat16)
    empty_state = (
        jnp.zeros((capacity, heads_here, HEAD), jnp.float32),
        jnp.zeros((capacity, heads_here), jnp.float32),
    )
    start_state = attend(empty_state, queries, query_tags, text_keys, text_values, text_tags)
    numerator, denominator = attend(
        start_state,
        queries,
        query_tags,
        lax.all_gather(key_rows, "patch", axis=0, tiled=True),
        lax.all_gather(value_rows, "patch", axis=0, tiled=True),
        lax.all_gather(key_tags, "patch", axis=0, tiled=True),
    )
    safe_denominator = denominator + (slot_item < 0).astype(jnp.float32)[:, None]
    attended = (
        (numerator / safe_denominator[:, :, None]).reshape(capacity, head_cols).astype(jnp.bfloat16)
    )
    head_part = jnp.dot(attended, w_out, preferred_element_type=jnp.float32)
    col_first = lax.axis_index("mlp") * share_cols
    attn_total = lax.psum(head_part, "mlp")
    after_attn = float_rows + slot_mods[:, 2] * attn_total
    normed_two = (layer_norm(after_attn) * (1.0 + slot_mods[:, 4]) + slot_mods[:, 3]).astype(
        jnp.bfloat16
    )
    up_total = jnp.dot(normed_two, w_up, preferred_element_type=jnp.float32)
    attn_share = lax.dynamic_slice_in_dim(after_attn, col_first, share_cols, 1)
    hidden_units = jax.nn.gelu(up_total, approximate=True).astype(jnp.bfloat16)
    unit_part = jnp.dot(hidden_units, w_down, preferred_element_type=jnp.float32)
    unit_total = lax.psum_scatter(unit_part, "mlp", scatter_dimension=1, tiled=True)
    gate_share = lax.dynamic_slice_in_dim(slot_mods[:, 5], col_first, share_cols, 1)
    after_mlp = attn_share + gate_share * unit_total
    next_rows = latent.astype(jnp.float32) + slot_step[:, None] * after_mlp
    return jnp.where(slot_live[:, None], next_rows, 0.0).astype(jnp.bfloat16)


def solution(mesh):
    return jax.shard_map(
        body,
        mesh=mesh,
        in_specs=(
            P("patch", "mlp"),
            P("patch", None),
            P(),
            P(None, None, "mlp"),
            P("mlp", None),
            P(None, "mlp"),
            P("mlp", None),
            P(),
            P(None, None, None, "mlp"),
            P(),
            P(),
        ),
        out_specs=P("patch", "mlp"),
        check_vma=False,
    )
```

profile of v0, /device:TPU:0, one launch (start us, length us, event | category | flops | bytes accessed | tf_op | source)
XLA Modules:
  0.0 319.1 jit_solution(8434744912893777445)
XLA Ops:
  15.4 6.1 %broadcast_multiply_fusion = f32[256,6,2432]{0,2,1:T(8,128)} fusion(f32[6,2432]{1,0:T(8,128)S(1)} %bitcast.153, f32[256]{0:T(256)S(1)} %get-tuple-element.424), kind=kLoop, calls=%fused_computation.23 | loop fusion | flops 3735552 | bytes 15001600 | tf_op jit(solution)/shard_map/dot_general | solution.py:104
  21.6 21.7 %all-gather.6.cloned.1.call-done = bf16[256,2432]{0,1:T(8,128)(2,1)} async-done(((bf16[256,608]{0,1:T(8,128)(2,1)}), bf16[256,2432]{0,1:T(8,128)(2,1)}) %all-gather.6.cloned.1.call-update) | async-done | bytes 1245200 | tf_op jit(solution)/shard_map/all_gather | solution.py:91
  46.7 6.0 %fusion.44 = f32[256,3,384]{2,0,1:T(8,128)S(1)} fusion(bf16[2432,3,384]{2,0,1:T(8,128)(2,1)} %param.20, f32[256,6,2432]{0,2,1:T(8,128)} %broadcast_multiply_fusion, bf16[256,2432]{0,1:T(8,128)(2,1)S(1)} %copy-done.2, f32[256]{0:T(256)S(1)} %add_rsqrt_fusion.4, f32[256]{0:T(256)S(1)} %broadcast_multiply_fusion.2), kind=kOutput, calls=%fused_computation.58 | convolution fusion | flops 1438810112 | bytes 13010944 | tf_op jit(solution)/shard_map/nd,dch->nch/dot_general | solution.py:120
  61.2 2.1 fusion.60
  75.1 2.6 reshape.303
  79.7 2.2 fusion.63
  81.9 2.6 mul.193
  86.5 2.1 copy.95
  88.7 9.0 %all-gather.1 = bf16[8,1,256]{2,1,0:T(2,128)(2,1)S(1)} all-gather(bf16[1,1,256]{2,1,0:T(2,128)(2,1)S(1)} %reshape.300), channel_id=1, replica_groups=mesh['patch'=8,'mlp'=4] {'patch'}, dimensions={0}, use_global_device_ids=true | all-gather | bytes 4608 | tf_op jit(solution)/shard_map/all_gather | solution.py:146
  100.5 8.4 %conditional.2 = (f32[256,6,64]{0,2,1:T(8,128)S(1)}, f32[256,6]{0,1:T(8,128)S(1)}) conditional(s32[]{:T(128)} %convert_element_type.111, () %tuple.38, (bf16[256]{0:T(256)(128)(2,1)S(1)}, s32[2]{0:T(128)S(1)}, bf16[308,384]{1,0:T(8,128)(2,1)}, bf16[256,384]{1,0:T(8,128)(2,1)S(1)}, bf16[2,2,154,384]{2,1,3,0:T(2,128)(2,1)}) %tuple.110), branch_computations={%region_5.6_spmd, %region_6.8_spmd} | conditional | flops 123080192 | bytes 5880796 | solution.py:55
  108.9 2.6 copy.105
  111.5 2.6 copy.103
  114.1 29.6 %while.17 = (s32[]{:T(128)}, f32[256,6,64]{0,2,1:T(8,128)S(1)}, f32[256,6]{0,1:T(8,128)S(1)}, bf16[2048]{0:T(1024)(128)(2,1)S(1)}, bf16[2048,384]{0,1:T(8,128)(2...) while((s32[]{:T(128)}, f32[256,6,64]{0,2,1:T(8,128)S(1)}, ...), condition=%wide.region_14.15_spmd.clone, body=%wide.region_9.14_spmd.clone.sunk | while | flops 206537984 | bytes 10057545 | solution.py:73
  117.6 3.9 %conditional.5 = ((f32[256,6,64]{0,2,1:T(8,128)S(1)}, f32[256,6]{0,1:T(8,128)S(1)})) conditional(s32[]{:T(128)} %convert_element_type.190, (f32[256,6,64]{0,2,1:T(8,128)S(1)}, f32[256,6]{0,1:T(8,128)S(1)}) %tuple.89, (bf16[256]{0:T(256)(128)(2,1)S(1)}, bf16[512]{0:T(512)(128)(2,1)S(1)}, bf16[2048,384]{0,1:T(8,128)(2,1)}, s32[]{:T(128)}, ...), branch_computations={%region_11.11_spmd, %region_12.13_spmd} | conditional | flops 206274560 | bytes 10053148 | solution.py:55
  125.0 3.9 %conditional.5 = ((f32[256,6,64]{0,2,1:T(8,128)S(1)}, f32[256,6]{0,1:T(8,128)S(1)})) conditional(s32[]{:T(128)} %convert_element_type.190, (f32[256,6,64]{0,2,1:T(8,128)S(1)}, f32[256,6]{0,1:T(8,128)S(1)}) %tuple.89, (bf16[256]{0:T(256)(128)(2,1)S(1)}, bf16[512]{0:T(512)(128)(2,1)S(1)}, bf16[2048,384]{0,1:T(8,128)(2,1)}, s32[]{:T(128)}, ...), branch_computations={%region_11.11_spmd, %region_12.13_spmd} | conditional | flops 206274560 | bytes 10053148 | solution.py:55
  132.4 3.9 %conditional.5 = ((f32[256,6,64]{0,2,1:T(8,128)S(1)}, f32[256,6]{0,1:T(8,128)S(1)})) conditional(s32[]{:T(128)} %convert_element_type.190, (f32[256,6,64]{0,2,1:T(8,128)S(1)}, f32[256,6]{0,1:T(8,128)S(1)}) %tuple.89, (bf16[256]{0:T(256)(128)(2,1)S(1)}, bf16[512]{0:T(512)(128)(2,1)S(1)}, bf16[2048,384]{0,1:T(8,128)(2,1)}, s32[]{:T(128)}, ...), branch_computations={%region_11.11_spmd, %region_12.13_spmd} | conditional | flops 206274560 | bytes 10053148 | solution.py:55
  139.8 3.9 %conditional.5 = ((f32[256,6,64]{0,2,1:T(8,128)S(1)}, f32[256,6]{0,1:T(8,128)S(1)})) conditional(s32[]{:T(128)} %convert_element_type.190, (f32[256,6,64]{0,2,1:T(8,128)S(1)}, f32[256,6]{0,1:T(8,128)S(1)}) %tuple.89, (bf16[256]{0:T(256)(128)(2,1)S(1)}, bf16[512]{0:T(512)(128)(2,1)S(1)}, bf16[2048,384]{0,1:T(8,128)(2,1)}, s32[]{:T(128)}, ...), branch_computations={%region_11.11_spmd, %region_12.13_spmd} | conditional | flops 206274560 | bytes 10053148 | solution.py:55
  143.8 2.4 fusion.75
  146.3 98.0 %all-reduce.2.cloned.1.call-done = f32[256,2432]{0,1:T(8,128)} async-done(((f32[256,2432]{0,1:T(8,128)}), f32[256,2432]{0,1:T(8,128)}) %all-reduce.2.cloned.1.call-update) | async-done | bytes 2490384 | tf_op jit(solution)/shard_map/psum | solution.py:154
  244.3 2.9 fusion.71
  249.0 12.0 %convolution_bitcast_fusion.1 = f32[2432,256]{1,0:T(8,128)} fusion(bf16[1280,2432]{1,0:T(8,128)(2,1)} %param.23, bf16[2432,1280]{1,0:T(8,128)(2,1)} %param.22, f32[256,6,2432]{0,2,1:T(8,128)} %broadcast_multiply_fusion, f32[256,2432]{0,1:T(8,128)} %copy-done.1, f32[256]{0:T(256)S(1)} %add_rsqrt_fusion.3, f32[256]{0:T(256)S(1)} %broadcast_multiply_fusion.1), kind=kOutput, calls=%fused_computation.24 | convolution fusion | flops 3194355712 | bytes 22415360
  261.0 3.4 %slice.85 = f32[256,1,2432]{0,2,1:T(8,128)} slice(f32[256,6,2432]{0,2,1:T(8,128)} %broadcast_multiply_fusion), slice={[0:256], [5:6], [0:2432]} | slice | bytes 4980736 | tf_op jit(solution)/shard_map/slice | solution.py:164
  264.4 45.9 %reduce-scatter.4.cloned.1.call-done = f32[608,256]{1,0:T(8,128)} async-done(((f32[2432,256]{1,0:T(8,128)}), f32[608,256]{1,0:T(8,128)}) %reduce-scatter.4.cloned.1.call-update) | async-done | bytes 622608
  310.3 2.3 fusion.58
  (122 shorter events, 70.9 us)
Async XLA Ops:
  6.5 137.3 %copy-start = (bf16[384,2432]{1,0:T(8,128)(2,1)S(1)}, bf16[384,2432]{1,0:T(8,128)(2,1)}, u32[]{:S(2)}) copy-start(bf16[384,2432]{1,0:T(8,128)(2,1)} %param.21) | copy-start | bytes 5603332
  6.5 36.7 %all-gather.6.cloned.1.call-start = ((), (), s32[]{:S(2)}) async-start(), calls=%async_computation.1 | async-start | bytes 1556480 | tf_op jit(solution)/shard_map/all_gather | solution.py:91
  7.3 101.7 %all-gather.10.cloned.1.call-start = ((), (), s32[]{:S(2)}) async-start(), calls=%async_computation.4 | async-start | bytes 1769472 | tf_op jit(solution)/shard_map/all_gather | solution.py:145
  43.2 3.4 %copy-start.2 = (bf16[256,2432]{0,1:T(8,128)(2,1)S(1)}, bf16[256,2432]{0,1:T(8,128)(2,1)}, u32[]{:S(2)}) copy-start(bf16[256,2432]{0,1:T(8,128)(2,1)} %all-gather.6.cloned.1.call-done) | copy-start | bytes 3735556
  46.7 7.9 %copy-start.7 = (f32[3,64]{1,0:T(4,128)S(1)}, f32[3,64]{1,0:T(4,128)}, u32[]{:S(2)}) copy-start(f32[3,64]{1,0:T(4,128)} %param.24) | copy-start | bytes 2308
  52.7 1.0 copy-start.4
  54.5 57.1 %all-gather.8.cloned.1.call-start = ((), (), s32[]{:S(2)}) async-start(), calls=%async_computation.2 | async-start | bytes 1769472 | tf_op jit(solution)/shard_map/all_gather | solution.py:144
  63.3 181.0 %all-reduce.2.cloned.1.call-start = ((), (), s32[]{:S(2)}) async-start(), calls=%async_computation.3 | async-start | bytes 4980736 | tf_op jit(solution)/shard_map/psum | solution.py:154
  72.9 0.9 copy-start.3
  106.6 1.7 copy-start.6
  146.3 164.0 %reduce-scatter.4.cloned.1.call-start = ((), (), s32[]{:S(2)}) async-start(), calls=%async_computation.5 | async-start | bytes 3112960
  247.2 1.4 copy-start.1
  261.0 49.3 %copy-start.5 = (bf16[256,608]{0,1:T(8,128)(2,1)S(1)}, bf16[256,608]{0,1:T(8,128)(2,1)}, u32[]{:S(2)}) copy-start(bf16[256,608]{0,1:T(8,128)(2,1)} %param.17) | copy-start | bytes 933892
Sparse Core Ops, SparseCore 0:
  8.9 34.2 all-gather.5
  54.6 24.7 all-gather.9
  81.3 25.7 all-gather.7
  146.4 97.8 all-reduce.1
  261.1 49.0 reduce-scatter.3
where the time goes:
time: 321 us; the launch traced here: 319 us
  waiting for transfers between devices  166 us (52%)
  local copies, waits for them, and re-layouts  45.1 us (14%)
  other arithmetic  44.3 us (14%)
  matrix products  32.5 us (10%)
  between operations  18.6 us (6%)
  blocking collectives  9.01 us (3%)
    psum x1, waiting for transfers between devices, body(): attn_total = lax.psum(head_part, 'mlp')  98 us
    unnamed x6, waiting for transfers between devices  46.6 us
    all_gather x1, waiting for transfers between devices, body(): row_data = lax.all_gather(latent, 'mlp', axis=1, tiled=True)  21.7 us
    unnamed x1, matrix products  12 us
    unnamed x20, local copies, waits for them, and re-layouts  10.3 us
    all_gather x1, blocking collectives, body(): lax.all_gather(key_tags, 'patch', axis=0, tiled=True)  9.01 us
    dot_general x5, matrix products, attend_dense(): jnp.einsum('qhd,khd->qhk', query_heads, key_heads, preferred_element_type...  8.96 us
    convert_element_type x4, other arithmetic, body(): query_tags = slot_item.astype(jnp.bfloat16)  7.74 us
  transfers between devices with their start and end apart: 5, of which 3 were waited for; matrix products, arithmetic and copies ran while one was open for 18% of the time, Pallas kernels for 0%

commit v1 on v0

--- a/solution.py
+++ b/solution.py
@@ -1,3 +1,4 @@
+import functools
 import jax
 import jax.numpy as jnp
 from jax import lax
@@ -6,6 +7,20 @@
 HEAD = 64
 norm_eps = 1e-06
 block_rows = 512
+
+
+def change_the_plane(local_array, axis_id):
+    lanes = jax.lax.axis_size(axis_id)
+    z2 = local_array
+    high = lambda last: [(d, d ^ last) for d in range(lanes)]
+    for m in range(lanes.bit_length() - 1):
+        built = high(1 << m)
+        v_now = jax.lax.ppermute(z2, axis_name=axis_id, perm=built)
+        z2 = z2 + v_now
+    return z2
+
+
+_show_copies = functools.partial(change_the_plane, axis_id="mlp")
 
 
 def layer_norm(row_data):
@@ -151,7 +166,7 @@
     )
     head_part = jnp.dot(attended, w_out, preferred_element_type=jnp.float32)
     col_first = lax.axis_index("mlp") * share_cols
-    attn_total = lax.psum(head_part, "mlp")
+    attn_total = _show_copies(head_part)
     after_attn = float_rows + slot_mods[:, 2] * attn_total
     normed_two = (layer_norm(after_attn) * (1.0 + slot_mods[:, 4]) + slot_mods[:, 3]).astype(
         jnp.bfloat16

time: 321 us -> 386 us (1.20)
  waiting for transfers between devices: 166 us -> 231 us
    ppermute x0 -> x2, waiting for transfers between devices: none -> 164 us  [change_the_plane(): v_now = jax.lax.ppermute(z2, axis_name=axis_id, perm=built)]
    psum x1 -> x0, waiting for transfers between devices: 98 us -> none  [body(): attn_total = lax.psum(head_part, 'mlp')]
    unnamed x6 -> x5, waiting for transfers between devices: 46.6 us -> 45.7 us
  transfers between devices with their start and end apart: 5 -> 6, of which waited for: 3 -> 4; matrix products, arithmetic and copies ran while one was open for 18% -> 15% of each run, Pallas kernels for 0% -> 0%
where the time goes in v1:
time: 386 us; the launch traced here: 384 us
  waiting for transfers between devices  231 us (60%)
  local copies, waits for them, and re-layouts  45.1 us (12%)
  other arithmetic  44.2 us (11%)
  matrix products  31.1 us (8%)
  between operations  18.5 us (5%)
  blocking collectives  8.8 us (2%)
    ppermute x2, waiting for transfers between devices, change_the_plane(): v_now = jax.lax.ppermute(z2, axis_name=axis_id, perm=built)  164 us
    unnamed x5, waiting for transfers between devices  45.7 us
    all_gather x1, waiting for transfers between devices, body(): row_data = lax.all_gather(latent, 'mlp', axis=1, tiled=True)  21.6 us
    unnamed x1, matrix products  12 us
    unnamed x20, local copies, waits for them, and re-layouts  10.3 us
    dot_general x5, matrix products, attend_dense(): jnp.einsum('qhd,khd->qhk', query_heads, key_heads, preferred_element_type...  8.96 us
    all_gather x1, blocking collectives, body(): lax.all_gather(key_tags, 'patch', axis=0, tiled=True)  8.8 us
  transfers between devices with their start and end apart: 6, of which 4 were waited for; matrix products, arithmetic and copies ran while one was open for 15% of the time, Pallas kernels for 0%

profile of v1, /device:TPU:0, one launch (start us, length us, event | category | flops | bytes accessed | tf_op | source)
XLA Modules:
  0.0 384.3 jit_solution(3827176584083084665)
XLA Ops:
  15.5 6.1 %broadcast_multiply_fusion = f32[256,6,2432]{0,2,1:T(8,128)} fusion(f32[6,2432]{1,0:T(8,128)S(1)} %bitcast.153, f32[256]{0:T(256)S(1)} %get-tuple-element.424), kind=kLoop, calls=%fused_computation.23 | loop fusion | flops 3735552 | bytes 15001600 | tf_op jit(solution)/shard_map/dot_general | solution.py:119
  21.6 21.6 %all-gather.6.cloned.1.call-done = bf16[256,2432]{0,1:T(8,128)(2,1)} async-done(((bf16[256,608]{0,1:T(8,128)(2,1)}), bf16[256,2432]{0,1:T(8,128)(2,1)}) %all-gather.6.cloned.1.call-update) | async-done | bytes 1245200 | tf_op jit(solution)/shard_map/all_gather | solution.py:106
  46.7 6.0 %fusion.44 = f32[256,3,384]{2,0,1:T(8,128)S(1)} fusion(bf16[2432,3,384]{2,0,1:T(8,128)(2,1)} %param.20, f32[256,6,2432]{0,2,1:T(8,128)} %broadcast_multiply_fusion, bf16[256,2432]{0,1:T(8,128)(2,1)S(1)} %copy-done.2, f32[256]{0:T(256)S(1)} %add_rsqrt_fusion.4, f32[256]{0:T(256)S(1)} %broadcast_multiply_fusion.2), kind=kOutput, calls=%fused_computation.58 | convolution fusion | flops 1438810112 | bytes 13010944 | tf_op jit(solution)/shard_map/nd,dch->nch/dot_general | solution.py:135
  61.2 2.1 fusion.60
  74.8 2.6 reshape.303
  79.5 2.2 fusion.63
  81.7 2.6 mul.193
  86.3 2.1 copy.95
  88.5 8.8 %all-gather.1 = bf16[8,1,256]{2,1,0:T(2,128)(2,1)S(1)} all-gather(bf16[1,1,256]{2,1,0:T(2,128)(2,1)S(1)} %reshape.300), channel_id=1, replica_groups=mesh['patch'=8,'mlp'=4] {'patch'}, dimensions={0}, use_global_device_ids=true | all-gather | bytes 4608 | tf_op jit(solution)/shard_map/all_gather | solution.py:161
  100.1 8.4 %conditional.2 = (f32[256,6,64]{0,2,1:T(8,128)S(1)}, f32[256,6]{0,1:T(8,128)S(1)}) conditional(s32[]{:T(128)} %convert_element_type.111, () %tuple.38, (bf16[256]{0:T(256)(128)(2,1)S(1)}, s32[2]{0:T(128)S(1)}, bf16[308,384]{1,0:T(8,128)(2,1)}, bf16[256,384]{1,0:T(8,128)(2,1)S(1)}, bf16[2,2,154,384]{2,1,3,0:T(2,128)(2,1)}) %tuple.108), branch_computations={%region_5.6_spmd, %region_6.8_spmd} | conditional | flops 123080192 | bytes 5880796 | solution.py:70
  108.5 2.6 copy.105
  111.1 2.6 copy.103
  113.7 29.6 %while.17 = (s32[]{:T(128)}, f32[256,6,64]{0,2,1:T(8,128)S(1)}, f32[256,6]{0,1:T(8,128)S(1)}, bf16[2048]{0:T(1024)(128)(2,1)S(1)}, bf16[2048,384]{0,1:T(8,128)(2...) while((s32[]{:T(128)}, f32[256,6,64]{0,2,1:T(8,128)S(1)}, ...), condition=%wide.region_14.15_spmd.clone, body=%wide.region_9.14_spmd.clone.sunk | while | flops 206537984 | bytes 10057545 | solution.py:88
  117.2 3.9 %conditional.5 = ((f32[256,6,64]{0,2,1:T(8,128)S(1)}, f32[256,6]{0,1:T(8,128)S(1)})) conditional(s32[]{:T(128)} %convert_element_type.190, (f32[256,6,64]{0,2,1:T(8,128)S(1)}, f32[256,6]{0,1:T(8,128)S(1)}) %tuple.89, (bf16[256]{0:T(256)(128)(2,1)S(1)}, bf16[512]{0:T(512)(128)(2,1)S(1)}, bf16[2048,384]{0,1:T(8,128)(2,1)}, s32[]{:T(128)}, ...), branch_computations={%region_11.11_spmd, %region_12.13_spmd} | conditional | flops 206274560 | bytes 10053148 | solution.py:70
  124.6 3.9 %conditional.5 = ((f32[256,6,64]{0,2,1:T(8,128)S(1)}, f32[256,6]{0,1:T(8,128)S(1)})) conditional(s32[]{:T(128)} %convert_element_type.190, (f32[256,6,64]{0,2,1:T(8,128)S(1)}, f32[256,6]{0,1:T(8,128)S(1)}) %tuple.89, (bf16[256]{0:T(256)(128)(2,1)S(1)}, bf16[512]{0:T(512)(128)(2,1)S(1)}, bf16[2048,384]{0,1:T(8,128)(2,1)}, s32[]{:T(128)}, ...), branch_computations={%region_11.11_spmd, %region_12.13_spmd} | conditional | flops 206274560 | bytes 10053148 | solution.py:70
  132.0 3.9 %conditional.5 = ((f32[256,6,64]{0,2,1:T(8,128)S(1)}, f32[256,6]{0,1:T(8,128)S(1)})) conditional(s32[]{:T(128)} %convert_element_type.190, (f32[256,6,64]{0,2,1:T(8,128)S(1)}, f32[256,6]{0,1:T(8,128)S(1)}) %tuple.89, (bf16[256]{0:T(256)(128)(2,1)S(1)}, bf16[512]{0:T(512)(128)(2,1)S(1)}, bf16[2048,384]{0,1:T(8,128)(2,1)}, s32[]{:T(128)}, ...), branch_computations={%region_11.11_spmd, %region_12.13_spmd} | conditional | flops 206274560 | bytes 10053148 | solution.py:70
  139.4 3.9 %conditional.5 = ((f32[256,6,64]{0,2,1:T(8,128)S(1)}, f32[256,6]{0,1:T(8,128)S(1)})) conditional(s32[]{:T(128)} %convert_element_type.190, (f32[256,6,64]{0,2,1:T(8,128)S(1)}, f32[256,6]{0,1:T(8,128)S(1)}) %tuple.89, (bf16[256]{0:T(256)(128)(2,1)S(1)}, bf16[512]{0:T(512)(128)(2,1)S(1)}, bf16[2048,384]{0,1:T(8,128)(2,1)}, s32[]{:T(128)}, ...), branch_computations={%region_11.11_spmd, %region_12.13_spmd} | conditional | flops 206274560 | bytes 10053148 | solution.py:70
  145.2 55.5 %collective-permute-done = f32[256,2432]{0,1:T(8,128)S(1)} collective-permute-done((f32[256,2432]{0,1:T(8,128)S(1)}, f32[256,2432]{0,1:T(8,128)S(1)}, u32[]{:S(2)}, u32[]{:S(2)}) %collective-permute-start) | collective-permute-done | bytes 2490400 | tf_op jit(solution)/shard_map/ppermute | solution.py:18
  202.5 108.3 %collective-permute-done.1 = f32[256,2432]{0,1:T(8,128)S(1)} collective-permute-done((f32[256,2432]{0,1:T(8,128)S(1)}, f32[256,2432]{0,1:T(8,128)S(1)}, u32[]{:S(2)}, u32[]{:S(2)}) %collective-permute-start.1) | collective-permute-done | bytes 2490400 | tf_op jit(solution)/shard_map/ppermute | solution.py:18
  310.8 2.4 fusion.71
  315.0 12.0 %convolution_bitcast_fusion.1 = f32[2432,256]{1,0:T(8,128)} fusion(bf16[1280,2432]{1,0:T(8,128)(2,1)} %param.23, bf16[2432,1280]{1,0:T(8,128)(2,1)} %param.22, f32[256,6,2432]{0,2,1:T(8,128)} %broadcast_multiply_fusion, f32[256,2432]{0,1:T(8,128)} %copy-done.1, f32[256]{0:T(256)S(1)} %add_rsqrt_fusion.3, f32[256]{0:T(256)S(1)} %broadcast_multiply_fusion.1), kind=kOutput, calls=%fused_computation.24 | convolution fusion | flops 3194355712 | bytes 22415360
  327.1 3.4 slice.85
  330.5 44.9 %reduce-scatter.4.cloned.1.call-done = f32[608,256]{1,0:T(8,128)} async-done(((f32[2432,256]{1,0:T(8,128)}), f32[608,256]{1,0:T(8,128)}) %reduce-scatter.4.cloned.1.call-update) | async-done | bytes 622608
  375.4 2.3 fusion.58
  (124 shorter events, 74.5 us)
Async XLA Ops:
  6.5 136.8 %copy-start = (bf16[384,2432]{1,0:T(8,128)(2,1)S(1)}, bf16[384,2432]{1,0:T(8,128)(2,1)}, u32[]{:S(2)}) copy-start(bf16[384,2432]{1,0:T(8,128)(2,1)} %param.21) | copy-start | bytes 5603332
  6.5 36.7 %all-gather.6.cloned.1.call-start = ((), (), s32[]{:S(2)}) async-start(), calls=%async_computation.1 | async-start | bytes 1556480 | tf_op jit(solution)/shard_map/all_gather | solution.py:106
  7.3 101.2 %all-gather.10.cloned.1.call-start = ((), (), s32[]{:S(2)}) async-start(), calls=%async_computation.3 | async-start | bytes 1769472 | tf_op jit(solution)/shard_map/all_gather | solution.py:160
  43.2 3.4 copy-start.2
  46.7 7.9 %copy-start.7 = (f32[3,64]{1,0:T(4,128)S(1)}, f32[3,64]{1,0:T(4,128)}, u32[]{:S(2)}) copy-start(f32[3,64]{1,0:T(4,128)} %param.24) | copy-start | bytes 2308
  52.7 1.0 copy-start.4
  54.5 56.6 %all-gather.8.cloned.1.call-start = ((), (), s32[]{:S(2)}) async-start(), calls=%async_computation.2 | async-start | bytes 1769472 | tf_op jit(solution)/shard_map/all_gather | solution.py:159
  63.3 312.1 %reduce-scatter.4.cloned.1.call-start = ((), (), s32[]{:S(2)}) async-start(), calls=%async_computation.4 | async-start | bytes 3112960
  72.7 0.9 copy-start.3
  106.2 1.8 copy-start.6
  144.3 56.3 %collective-permute-start = (f32[256,2432]{0,1:T(8,128)S(1)}, f32[256,2432]{0,1:T(8,128)S(1)}, u32[]{:S(2)}, u32[]{:S(2)}) collective-permute-start(f32[256,2432]{0,1:T(8,128)S(1)} %fusion.75), channel_id=1, source_target_pairs={{0,1},{1,0},{2,3},{3,2},{4,5},{5,4},{6,7},{7,6},{8,9},{9,8},{10,11... | collective-permute-start | bytes 7471112 | tf_op jit(solution)/shard_map/ppermute | solution.py:18
  201.0 109.8 %collective-permute-start.1 = (f32[256,2432]{0,1:T(8,128)S(1)}, f32[256,2432]{0,1:T(8,128)S(1)}, u32[]{:S(2)}, u32[]{:S(2)}) collective-permute-start(f32[256,2432]{0,1:T(8,128)S(1)} %add.170), channel_id=1, source_target_pairs={{0,2},{1,3},{2,0},{3,1},{4,6},{5,7},{6,4},{7,5},{8,10},{9,11},{10,... | collective-permute-start | bytes 7471112 | tf_op jit(solution)/shard_map/ppermute | solution.py:18
  313.2 1.4 copy-start.1
  327.1 48.3 %copy-start.5 = (bf16[256,608]{0,1:T(8,128)(2,1)S(1)}, bf16[256,608]{0,1:T(8,128)(2,1)}, u32[]{:S(2)}) copy-start(bf16[256,608]{0,1:T(8,128)(2,1)} %param.17) | copy-start | bytes 933892
Sparse Core Ops, SparseCore 0:
  8.9 34.2 all-gather.5
  54.6 24.7 all-gather.9
  81.3 25.6 all-gather.7
  327.2 48.1 reduce-scatter.3
